TPU v7x, 32 devices: a whole 2x2x4 slice. The times are simulated.
32 devices in a mesh: wind: 4 (over z), state: 8 (over y, x, core).
Axes of the slice: x: 2, y: 2, z: 4, core: 2. Of those that a mesh axis runs over, the one named last changes fastest.
Arguments:
- value_next: float32 [128, 16, 256, 256], P('wind', None, 'state'), may hold values from -6 to 6
- density: float32 [128, 16, 256, 256], P('wind', None, 'state'), may hold values from 0.1 to 2
- price: float32 [128, 16], P('wind'), may hold values from -4 to 4
- wind_rate: float32 [128, 16], P('wind'), may hold values from 0.05 to 0.5
- tank_inverse: float32 [256, 256], replicated, may hold values from -0.5 to 1.5
- soc_inverse: float32 [256, 256], replicated, may hold values from -0.5 to 1.5
Outputs:
- value: float32 [128, 16, 256, 256], P('wind', None, 'state')
- density_next: float32 [128, 16, 256, 256], P('wind', None, 'state')
All inputs are finite; a program needn't handle non-finite values.
Results may differ from a plain program's by a relative error of at most 0.0001.
Values sent between devices are 32-bit elements; how exact they have to be, the bound alone decides.
No kernel may reach another device: no remote copies, remote signals or barrier semaphores. Data moves between devices by JAX's collectives and lax.ppermute only.
A program may use at most 320 MiB of HBM per device.

v0:
```python
import functools

import jax
import jax.numpy as jnp
from jax import lax
from jax.experimental import pallas as pl
from jax.experimental.pallas import tpu as pltpu
from jax.sharding import PartitionSpec as P

ITERS = 4
HALO = ITERS
LANES = 128
PIECE = 6
SHARES = (2, 3, 4, 4, 3)

step_size = 0.25
control_bound = 2.0
control_cost = 1.0
tank_spread = 0.3

MIB = 1 << 20
VMEM_LIMIT = 60 * MIB
TOKEN = jax.ShapeDtypeStruct((8, LANES), jnp.float32)


def split_parts(x):
    high = x.astype(jnp.bfloat16)
    low = (x - high.astype(jnp.float32)).astype(jnp.bfloat16)
    return high, low


def product(high, low, weight_high, weight_low):
    dot = functools.partial(jnp.dot, preferred_element_type=jnp.float32)
    return dot(high, weight_high) + (dot(low, weight_high) + dot(high, weight_low))


def half_shifted(slope4, price_half):
    return 0.25 * slope4 + price_half


def swap_groups(tiles, group):
    count = len(tiles)
    lane = lax.broadcasted_iota(jnp.int32, tiles[0].shape, len(tiles[0].shape) - 1)
    axis = len(tiles[0].shape) - 1
    bit = 1
    while bit < count:
        mine = (lane // group) & bit
        fresh = []
        for w in range(count):
            other = tiles[w ^ bit]
            if w & bit:
                rolled = pltpu.roll(other, LANES - bit * group, axis)
                fresh.append(jnp.where(mine != 0, tiles[w], rolled))
            else:
                rolled = pltpu.roll(other, bit * group, axis)
                fresh.append(jnp.where(mine == 0, tiles[w], rolled))
        tiles = fresh
        bit *= 2
    return tiles


def sweep_kernel(
    first_room, n, extra, info, price, rate, v, wl, wr, sl, sr, tank, *rest
):
    rest = rest[extra:]
    out, token, sends = rest[0], rest[1], rest[2 : 2 + n]
    base, field_a, field_b, x_high, x_low, t_high, t_low, stage = rest[2 + n :]
    token[...] = jnp.zeros(token.shape, token.dtype)
    planes, rows, cols = v.shape[0], v.shape[2], v.shape[3]
    wide = planes + 2 * HALO
    full = rows + 2 * HALO
    step = pl.program_id(0)
    room = first_room + step
    rooms = price.shape[0] // wide
    me = info[0]

    @pl.when(step == 0)
    def _():
        high, low = split_parts(tank[...])
        t_high[...] = high
        t_low[...] = low

    for p in range(HALO):
        base[p] = wl[p, 0]
        base[HALO + planes + p] = wr[p, 0]
    for p in range(planes):
        base[HALO + p, :rows] = v[p, 0]
        base[HALO + p, rows : rows + HALO] = sr[p, 0]
        base[HALO + p, rows + HALO :] = sl[p, 0]

    source = base
    for sweep in range(ITERS):
        last = sweep == ITERS - 1
        begin = sweep + 1
        count = wide - 2 * begin
        kept = rows if last else full
        target = (field_a, field_b)[sweep % 2]

        def one(p, source=source, kept=kept):
            u = source[p]
            above = pltpu.roll(u, full - 1, 0)
            below = pltpu.roll(u, 1, 0)
            scalar = p * rooms + room
            y = (0.25 * (above - below))[:kept] + 0.5 * price[scalar]
            t = jnp.tanh(y)
            r = step_size * rate[scalar]
            sides = source[p + 1, :kept] + source[p - 1, :kept]
            return (
                base[p, :kept]
                + t * (0.5 * t - y)
                + r * (sides - 2.0 * u[:kept])
            )

        done = 0
        while done < count:
            size = min(PIECE, count - done)
            for i in range(done, done + size, 2):
                both = jnp.concatenate([one(begin + i), one(begin + i + 1)], axis=0)
                high, low = split_parts(both)
                x_high[i * kept : (i + 2) * kept] = high
                x_low[i * kept : (i + 2) * kept] = low
            at = slice(done * kept, (done + size) * kept)
            u = product(x_high[at], x_low[at], t_high[...], t_low[...])
            u = u.reshape(size, kept, cols)
            if last:
                out[done : done + size, 0] = u
            else:
                target[begin + done : begin + done + size] = u
            done += size
        if not last:
            @pl.when(info[1] == 0)
            def _(target=target):
                target[HALO - 1] = jnp.zeros((full, cols), jnp.float32)

            @pl.when(info[2] == 0)
            def _(target=target):
                target[HALO + planes] = jnp.zeros((full, cols), jnp.float32)

            @pl.when(info[3] == 0)
            def _(target=target):
                target[:, rows + HALO :] = jnp.zeros((wide, HALO, cols), jnp.float32)

            @pl.when(info[4] == 0)
            def _(target=target):
                target[:, rows : rows + HALO] = jnp.zeros((wide, HALO, cols), jnp.float32)
        source = target

    width = cols // n
    per_tile = LANES // width

    def pack(g, carry):
        for tile in range(cols // LANES):
            at = slice(tile * LANES, (tile + 1) * LANES)
            tiles = [out[g * per_tile + w, 0, :, at] for w in range(per_tile)]
            tiles = swap_groups(tiles, width)
            for j in range(per_tile):
                stage[tile * per_tile + j, g] = tiles[j]
        return carry

    lax.fori_loop(0, planes // per_tile, pack, 0, unroll=True)
    for d in range(n):
        sends[d][0] = stage[jnp.bitwise_xor(me, d)]


def density_kernel(first_room, n, extra, info, price, rate, dens, wl, wr, kl, kr, soc, *rest):
    takes = rest[:n]
    rest = rest[n + extra :]
    out, token = rest[0], rest[1]
    column, level, x_high, x_low, g_high, g_low, m_high, m_low, q_high, q_low = rest[2:]
    token[...] = jnp.zeros(token.shape, token.dtype)
    planes, rows, cols = dens.shape[0], dens.shape[2], dens.shape[3]
    step = pl.program_id(0)
    room = first_room + step
    rooms = rate.shape[0] // planes
    me = info[0]
    per_tile = LANES // rows
    inner = takes[0].shape[2]

    @pl.when(step == 0)
    def _():
        m = soc[...]
        high, low = split_parts(m)
        m_high[...] = high
        m_low[...] = low
        line = lax.broadcasted_iota(jnp.int32, m.shape, 0)
        before = jnp.where(line == 0, 0.0, pltpu.roll(m, 1, 0))
        after = jnp.where(line == cols - 1, 0.0, pltpu.roll(m, cols - 1, 0))
        high, low = split_parts(step_size * (before - after))
        q_high[...] = high
        q_low[...] = low
        column[:, :8] = jnp.zeros((2, 8, LANES), jnp.float32)
        column[:, 8 + cols :] = jnp.zeros((2, 8, LANES), jnp.float32)

    for g in range(planes // per_tile):
        for d in range(n):
            at = pl.multiple_of(8 + inner * jnp.bitwise_xor(me, d), 8)
            column[g % 2, pl.ds(at, inner)] = takes[d][0, g]
        lane = lax.broadcasted_iota(jnp.int32, (1, LANES), 1)
        half_price = jnp.zeros((1, LANES), jnp.float32)
        for w in range(per_tile):
            scalar = 0.5 * price[(g * per_tile + w) * rooms + room]
            half_price = jnp.where(lane // rows == w, scalar, half_price)
        spot = column.at[g % 2]
        y = 0.25 * (spot[9 : 9 + cols] - spot[7 : 7 + cols]) + half_price
        t = jnp.tanh(y).T
        for w in range(per_tile):
            p = g * per_tile + w
            here = dens[p, 0]
            line = level.at[w % 2]
            line[8 : 8 + rows] = here
            line[7:8] = kl[p // HALO, 0, p % HALO : p % HALO + 1]
            line[8 + rows : 9 + rows] = kr[p // HALO, 0, p % HALO : p % HALO + 1]
            r = step_size * rate[p * rooms + room]
            wind_low = wl[0, 0, :rows] if p == 0 else dens[p - 1, 0]
            wind_up = wr[0, 0, :rows] if p == planes - 1 else dens[p + 1, 0]
            tank = line[7 : 7 + rows] + line[9 : 9 + rows] - 2.0 * here
            x = here + (step_size * tank_spread) * tank + r * (wind_up + wind_low - 2.0 * here)
            at = slice(p * rows, (p + 1) * rows)
            high, low = split_parts(x)
            x_high[at, :] = high
            x_low[at, :] = low
            high, low = split_parts(t[w * rows : (w + 1) * rows] * here)
            g_high[at, :] = high
            g_low[at, :] = low

    half = planes // 2
    for piece in range(2):
        at = pl.ds(piece * half * rows, half * rows)
        u = product(x_high[at, :], x_low[at, :], m_high[...], m_low[...])
        u += product(g_high[at, :], g_low[at, :], q_high[...], q_low[...])
        out[piece * half : (piece + 1) * half, 0] = u.reshape(half, rows, cols)


def smem():
    return pl.BlockSpec(memory_space=pltpu.SMEM)


def whole(shape):
    return pl.BlockSpec(shape, lambda i: (0,) * len(shape))


def room_block(planes, rows, cols, first=0):
    return pl.BlockSpec((planes, 1, rows, cols), lambda i: (0, first + i, 0, 0))


def run_sweeps(first, size, n, info, price, rate, value, halos, offsets, tank, previous, after):
    planes, rooms, rows, cols = value.shape
    wide, full = planes + 2 * HALO, rows + 2 * HALO
    groups = planes // (LANES // (cols // n))
    in_specs = [
        smem(),
        smem(),
        smem(),
        room_block(planes, rows, cols, first),
        room_block(HALO, full, cols, offsets[0]),
        room_block(HALO, full, cols, offsets[0]),
        room_block(planes, HALO, cols, offsets[1]),
        room_block(planes, HALO, cols, offsets[1]),
        whole((cols, cols)),
    ]
    args = [info, price, rate, value, *halos, tank]
    aliases = {}
    if first > 0:
        aliases = {len(args): 0}
        args.append(previous)
        in_specs.append(pl.BlockSpec(memory_space=pl.ANY))
    in_specs += [pl.BlockSpec(memory_space=pl.ANY)] * len(after)
    extra = (first > 0) + len(after)
    args += after
    packed = jax.ShapeDtypeStruct((size, groups, rows, LANES), jnp.float32)
    most = (wide - 2) * full
    flops = size * 2 * 3 * most * ITERS * cols * cols
    return pl.pallas_call(
        functools.partial(sweep_kernel, first, n, extra),
        grid=(size,),
        in_specs=in_specs,
        out_specs=[room_block(planes, rows, cols, first), whole(TOKEN.shape)]
        + [pl.BlockSpec((1, groups, rows, LANES), lambda i: (i, 0, 0, 0))] * n,
        out_shape=[jax.ShapeDtypeStruct(value.shape, jnp.float32), TOKEN] + [packed] * n,
        scratch_shapes=[
            pltpu.VMEM((wide, full, cols), jnp.float32),
            pltpu.VMEM((wide, full, cols), jnp.float32),
            pltpu.VMEM((wide, full, cols), jnp.float32),
            pltpu.VMEM((most, cols), jnp.bfloat16),
            pltpu.VMEM((most, cols), jnp.bfloat16),
            pltpu.VMEM((cols, cols), jnp.bfloat16),
            pltpu.VMEM((cols, cols), jnp.bfloat16),
            pltpu.VMEM((n, groups, rows, LANES), jnp.float32),
        ],
        input_output_aliases=aliases,
        compiler_params=pltpu.CompilerParams(vmem_limit_bytes=VMEM_LIMIT),
        cost_estimate=pl.CostEstimate(
            flops=flops, bytes_accessed=size * planes * rows * cols * 12, transcendentals=size * most * ITERS * cols
        ),
        name="sweeps",
    )(*args)


def run_density(first, size, n, info, price, rate, density, halos, offsets, soc, takes, previous, after):
    planes, rooms, rows, cols = density.shape
    groups = planes // (LANES // rows)
    inner = cols // n
    in_specs = [
        smem(),
        smem(),
        smem(),
        room_block(planes, rows, cols, first),
        pl.BlockSpec((1, 1, rows + 2 * HALO, cols), lambda i: (HALO, offsets[0] + i, 0, 0)),
        pl.BlockSpec((1, 1, rows + 2 * HALO, cols), lambda i: (HALO, offsets[0] + i, 0, 0)),
        pl.BlockSpec((planes // HALO, 1, HALO, cols), lambda i: (HALO, offsets[1] + i, 0, 0)),
        pl.BlockSpec((planes // HALO, 1, HALO, cols), lambda i: (HALO, offsets[1] + i, 0, 0)),
        whole((cols, cols)),
    ] + [pl.BlockSpec((1, groups, inner, LANES), lambda i: (i, 0, 0, 0))] * n
    args = [info, price, rate, density, *halos, soc, *takes]
    aliases = {}
    if first > 0:
        aliases = {len(args): 0}
        args.append(previous)
        in_specs.append(pl.BlockSpec(memory_space=pl.ANY))
    in_specs += [pl.BlockSpec(memory_space=pl.ANY)] * len(after)
    extra = (first > 0) + len(after)
    args += after
    most = planes * rows
    return pl.pallas_call(
        functools.partial(density_kernel, first, n, extra),
        grid=(size,),
        in_specs=in_specs,
        out_specs=[room_block(planes, rows, cols, first), whole(TOKEN.shape)],
        out_shape=[jax.ShapeDtypeStruct(density.shape, jnp.float32), TOKEN],
        scratch_shapes=[
            pltpu.VMEM((2, cols + 16, LANES), jnp.float32),
            pltpu.VMEM((2, rows + 16, cols), jnp.float32),
        ]
        + [pltpu.VMEM((most, cols), jnp.bfloat16)] * 4
        + [pltpu.VMEM((cols, cols), jnp.bfloat16)] * 4,
        input_output_aliases=aliases,
        compiler_params=pltpu.CompilerParams(vmem_limit_bytes=VMEM_LIMIT),
        cost_estimate=pl.CostEstimate(
            flops=size * 2 * 6 * most * cols * cols,
            bytes_accessed=size * most * cols * 12,
            transcendentals=size * most * cols,
        ),
        name="density",
    )(*args)


def neighbours(head, tail, axis):
    ends = lax.axis_size(axis) - 1
    before = lax.ppermute(tail, axis, [(i, i + 1) for i in range(ends)])
    after = lax.ppermute(head, axis, [(i + 1, i) for i in range(ends)])
    return before, after


def held(x, token):
    return x if token is None else x + token[0, 0]


def row_groups(edge):
    planes, rooms, cols = edge.shape
    return jnp.swapaxes(edge.reshape(planes // HALO, HALO, rooms, cols), 1, 2)


def state_halos(value, density, first, size):
    part, other = value[:, first : first + size], density[:, first : first + size]
    last = part.shape[2]
    head = jnp.concatenate([part[:, :, :HALO], row_groups(other[:, :, 0])], axis=0)
    tail = jnp.concatenate([part[:, :, last - HALO :], row_groups(other[:, :, last - 1])], axis=0)
    return neighbours(head, tail, "state")


def wind_halos(value, density, first, size, sides, token, extra=None):
    planes = value.shape[0]
    before, after = sides
    room = slice(first, first + size)
    ends = []
    for at, edge in ((slice(0, HALO), 0), (slice(planes - HALO, planes), planes - 1)):
        own = held(value[at, room], token)
        end = jnp.concatenate([own, after[at], before[at]], axis=2)
        other = jnp.pad(density[edge : edge + 1, room], ((0, 0), (0, 0), (0, 2 * HALO), (0, 0)))
        end = jnp.concatenate([end, other], axis=0)
        if extra is not None:
            end = jnp.concatenate([end, jnp.pad(extra[at], ((0, 1), (0, 0), (0, 0), (0, 0)))], axis=1)
        ends.append(end)
    return neighbours(ends[0], ends[1], "wind")


def chunk_sizes(rooms):
    shares = SHARES
    if rooms % sum(shares):
        return [1] * rooms
    return [rooms // sum(shares) * share for share in shares]


def on_device(value_next, density, price, wind_rate, tank_inverse, soc_inverse):
    planes, rooms, rows, cols = value_next.shape
    n = lax.axis_size("state")
    me = lax.axis_index("state")
    at = lax.axis_index("wind")
    info = jnp.stack(
        [me, at, lax.axis_size("wind") - 1 - at, me, n - 1 - me]
    ).astype(jnp.int32)
    sizes = chunk_sizes(rooms)
    starts = [sum(sizes[:c]) for c in range(len(sizes))]
    chunks = len(sizes)

    pair = jnp.stack([price, wind_rate], axis=1)
    slot = jnp.pad(pair[:, None], ((0, 0), (0, 0), (0, rows + 2 * HALO - 2), (0, cols - rooms)))
    price_flat, rate_flat = price.reshape(-1), wind_rate.reshape(-1)
    tank, soc = tank_inverse.T, soc_inverse.T

    sweep_done, density_done, takes = {}, {}, {}
    value, density_next = None, None

    early = sum(sizes[:2])
    later = rooms - early
    first_sides = state_halos(value_next, density, 0, early)
    later_sides = state_halos(value_next, density, early, later)

    def winds(first, size, sides, at, token, extra=None):
        sides = [x[:, at : at + size] for x in sides]
        return wind_halos(value_next, density, first, size, sides, token, extra)

    first_winds = winds(0, sizes[0], first_sides, 0, None, slot)
    wl, wr = first_winds
    wide = jnp.concatenate([wl[:HALO, sizes[0], :2, :rooms], pair, wr[:HALO, sizes[0], :2, :rooms]], axis=0)
    price_wide, rate_wide = wide[:, 0].reshape(-1), wide[:, 1].reshape(-1)
    second_winds = winds(sizes[0], sizes[1], first_sides, sizes[0], None)
    later_winds = winds(early, later, later_sides, 0, 0.0 * second_winds[0][0, 0])

    def halos_of(c):
        if c == 0:
            return first_winds + first_sides, (0, 0)
        if c == 1:
            return second_winds + first_sides, (0, sizes[0])
        return later_winds + later_sides, (starts[c] - early,) * 2

    def step(c):
        nonlocal density_next
        density_next, density_done[c] = run_density(
            starts[c], sizes[c], n, info, price_flat, rate_flat, density, *halos_of(c), soc, takes[c],
            density_next, [sweep_done[c + 1]] if c + 1 < chunks else [],
        )

    for c in range(chunks):
        first, size = starts[c], sizes[c]
        value, sweep_done[c], *sends = run_sweeps(
            first, size, n, info, price_wide, rate_wide, value_next,
            *halos_of(c), tank, value,
            [density_done[c - 2]] if c > 1 else [],
        )
        takes[c] = [sends[0]] * n
        for d in sorted(range(1, n), key=lambda d: (-(d >> 1).bit_count(), d)):
            takes[c][d] = lax.ppermute(sends[d], "state", [(i, i ^ d) for i in range(n)])
        if c > 0:
            step(c - 1)
    step(chunks - 1)
    return value, density_next


def solution(mesh):
    field = P("wind", None, "state", None)
    placed = (field, field, P("wind", None), P("wind", None), P(), P())
    return jax.shard_map(
        on_device,
        mesh=mesh,
        in_specs=placed,
        out_specs=(field, field),
        check_vma=False,
    )
```

profile of v0, /device:TPU:25, one launch (start us, length us, event | category | flops | bytes accessed | tf_op | source)
XLA Modules:
  0.0 328.0 jit_solution(7802862990634019990)
XLA Ops:
  0.6 2.0 fusion.13
  2.7 2.0 fusion.12
  5.8 3.7 %collective-permute-start.1 = (f32[40,5,4,256]{3,2,1,0:T(4,128)}, f32[40,5,4,256]{3,2,1,0:T(4,128)S(1)}, u32[]{:S(2)}, u32[]{:S(2)}) collective-permute-start(f32[40,5,4,256]{3,2,1,0:T(4,128)} %pad_maximum_fusion.3), channel_id=1, source_target_pairs={{0,1},{1,2},{2,3},{3,4},{4,5},{5,6},{6,7},{8,9},{9,10},{10,11},{11... | collective-permute-start | bytes 2457608 | tf_op jit(solution)/shard_map/ppermute | solution.py:349
  10.7 1.9 collective-permute-start
  12.6 3.2 fusion.9
  15.8 3.2 fusion.8
  21.0 3.6 %collective-permute-start.6 = (f32[40,11,4,256]{3,2,1,0:T(4,128)}, f32[40,11,4,256]{3,2,1,0:T(4,128)S(1)}, u32[]{:S(2)}, u32[]{:S(2)}) collective-permute-start(f32[40,11,4,256]{3,2,1,0:T(4,128)} %pad_maximum_fusion.1), channel_id=1, source_target_pairs={{0,1},{1,2},{2,3},{3,4},{4,5},{5,6},{6,7},{8,9},{9,10},{10,11},{11... | collective-permute-start | bytes 5406728 | tf_op jit(solution)/shard_map/ppermute | solution.py:349
  26.6 1.9 collective-permute-start.5
  41.2 5.4 %collective-permute-start.3 = (f32[5,3,40,256]{3,2,1,0:T(8,128)}, f32[5,3,40,256]{3,2,1,0:T(8,128)}, u32[]{:S(2)}, u32[]{:S(2)}) collective-permute-start(f32[5,3,40,256]{3,2,1,0:T(8,128)} %fusion), channel_id=1, source_target_pairs={{8,0},{16,8},{24,16},{9,1},{17,9},{25,17},{10,2},{18,10},{26,18},{... | collective-permute-start | bytes 1843208 | tf_op jit(solution)/shard_map/ppermute | solution.py:350
  54.1 2.1 collective-permute-start.9
  57.6 8.1 %collective-permute-done.2.wl = f32[5,3,40,256]{3,2,1,0:T(8,128)} collective-permute-done((f32[5,3,40,256]{3,2,1,0:T(8,128)}, f32[5,3,40,256]{3,2,1,0:T(8,128)}, u32[]{:S(2)}, u32[]{:S(2)}) %collective-permute-start.2) | collective-permute-done | bytes 614432 | tf_op jit(solution)/shard_map/ppermute | solution.py:349
  67.4 2.8 slice_add_fusion
  76.4 5.5 %collective-permute-start.8 = (f32[5,11,40,256]{3,2,1,0:T(8,128)}, f32[5,11,40,256]{3,2,1,0:T(8,128)}, u32[]{:S(2)}, u32[]{:S(2)}) collective-permute-start(f32[5,11,40,256]{3,2,1,0:T(8,128)} %select_maximum_fusion), channel_id=1, source_target_pairs={{8,0},{16,8},{24,16},{9,1},{17,9},{25,17},{10,2},{18,10},{26,18},{... | collective-permute-start | bytes 6758408 | tf_op jit(solution)/shard_map/ppermute | solution.py:350
  83.3 13.7 %sweeps.5 = (f32[32,16,32,256]{3,2,1,0:T(8,128)}, f32[8,128]{1,0:T(8,128)}, f32[2,8,32,128]{3,2,1,0:T(8,128)}, f32[2,8,32,128]{3,2,1,0:T(8,128)}, f32[2,8,32,128...) custom-call(s32[5]{0:T(128)} %stack.29.info, ...), custom_call_target="tpu_custom_call" | custom-call | flops 4781506560 | bytes 6291456 | tf_op jit(solution)/shard_map/sweeps/pallas_call | solution.py:273
  97.1 4.6 %collective-permute-start.11 = (f32[2,8,32,128]{3,2,1,0:T(8,128)}, f32[2,8,32,128]{3,2,1,0:T(8,128)}, u32[]{:S(2)}, u32[]{:S(2)}) collective-permute-start(f32[2,8,32,128]{3,2,1,0:T(8,128)} %get-tuple-element.63), channel_id=1, source_target_pairs={{0,2},{1,3},{2,0},{3,1},{4,6},{5,7},{6,4},{7,5},{8,10},{9,11},{10,... | collective-permute-start | bytes 786440 | tf_op jit(solution)/shard_map/ppermute | solution.py:453
  102.6 6.0 %collective-permute-done.11.rest_2_ = f32[2,8,32,128]{3,2,1,0:T(8,128)} collective-permute-done((f32[2,8,32,128]{3,2,1,0:T(8,128)}, f32[2,8,32,128]{3,2,1,0:T(8,128)}, u32[]{:S(2)}, u32[]{:S(2)}) %collective-permute-start.11) | collective-permute-done | bytes 262176 | tf_op jit(solution)/shard_map/ppermute | solution.py:453
  110.3 4.2 %collective-permute-done.12.rest_3_ = f32[2,8,32,128]{3,2,1,0:T(8,128)} collective-permute-done((f32[2,8,32,128]{3,2,1,0:T(8,128)}, f32[2,8,32,128]{3,2,1,0:T(8,128)}, u32[]{:S(2)}, u32[]{:S(2)}) %collective-permute-start.12) | collective-permute-done | bytes 262176 | tf_op jit(solution)/shard_map/ppermute | solution.py:453
  117.2 19.2 %sweeps.6 = (f32[32,16,32,256]{3,2,1,0:T(8,128)}, f32[8,128]{1,0:T(8,128)}, f32[3,8,32,128]{3,2,1,0:T(8,128)}, f32[3,8,32,128]{3,2,1,0:T(8,128)}, f32[3,8,32,128...) custom-call(s32[5]{0:T(128)} %stack.29.info, ...), custom_call_target="tpu_custom_call", output_to_operand_aliasing={{0}: (9, {})} | custom-call | flops 7172259840 | bytes 9437184 | tf_op jit(solution)/shard_map/sweeps/pallas_call | solution.py:273
  142.7 6.3 %density.5 = (f32[32,16,32,256]{3,2,1,0:T(8,128)}, f32[8,128]{1,0:T(8,128)}) custom-call(s32[5]{0:T(128)} %stack.29.info, f32[512]{0:T(512)} %reshape.12.price, f32[512]{0:T(512)} %reshape.13.rate, f32[32,16,32,256]{3,2,1,0:T(8,128)} %dens.9, f32[5,3,40,256]{3,2,1,0:T(8,128)} %collective-permute-done.2.wl, f32[5,3,40,256]{3,2,1,0:T(8,128)} %collective-permute-done.3.wr, ...), custom_call_target="tpu_custom_call" | custom-call | flops 1610612736 | bytes 6291456 | tf_op jit(solution)/shard_map/density/pallas_call | solution.py:324
  153.5 24.7 %sweeps.7 = (f32[32,16,32,256]{3,2,1,0:T(8,128)}, f32[8,128]{1,0:T(8,128)}, f32[4,8,32,128]{3,2,1,0:T(8,128)}, f32[4,8,32,128]{3,2,1,0:T(8,128)}, f32[4,8,32,128...) custom-call(s32[5]{0:T(128)} %stack.29.info, ...), custom_call_target="tpu_custom_call", output_to_operand_aliasing={{0}: (9, {})} | custom-call | flops 9563013120 | bytes 12582912 | tf_op jit(solution)/shard_map/sweeps/pallas_call | solution.py:273
  179.7 6.0 %collective-permute-done.21.rest_5_ = f32[3,8,32,128]{3,2,1,0:T(8,128)} collective-permute-done((f32[3,8,32,128]{3,2,1,0:T(8,128)}, f32[3,8,32,128]{3,2,1,0:T(8,128)}, u32[]{:S(2)}, u32[]{:S(2)}) %collective-permute-start.21) | collective-permute-done | bytes 393248 | tf_op jit(solution)/shard_map/ppermute | solution.py:453
  189.1 8.0 %density.6 = (f32[32,16,32,256]{3,2,1,0:T(8,128)}, f32[8,128]{1,0:T(8,128)}) custom-call(s32[5]{0:T(128)} %stack.29.info, f32[512]{0:T(512)} %reshape.12.price, f32[512]{0:T(512)} %reshape.13.rate, f32[32,16,32,256]{3,2,1,0:T(8,128)} %dens.9, f32[5,3,40,256]{3,2,1,0:T(8,128)} %collective-permute-done.4.wl, ...), custom_call_target="tpu_custom_call", output_to_operand_aliasing={{0}: (17, {})} | custom-call | flops 2415919104 | bytes 9437184 | tf_op jit(solution)/shard_map/density/pallas_call | solution.py:324
  197.5 2.0 collective-permute-start.30
  199.5 25.1 %sweeps.8 = (f32[32,16,32,256]{3,2,1,0:T(8,128)}, f32[8,128]{1,0:T(8,128)}, f32[4,8,32,128]{3,2,1,0:T(8,128)}, f32[4,8,32,128]{3,2,1,0:T(8,128)}, f32[4,8,32,128...) custom-call(s32[5]{0:T(128)} %stack.29.info, ...), custom_call_target="tpu_custom_call", output_to_operand_aliasing={{0}: (9, {})} | custom-call | flops 9563013120 | bytes 12582912 | tf_op jit(solution)/shard_map/sweeps/pallas_call | solution.py:273
  225.4 9.5 %collective-permute-done.28.rest_5_ = f32[4,8,32,128]{3,2,1,0:T(8,128)S(1)} collective-permute-done((f32[4,8,32,128]{3,2,1,0:T(8,128)}, f32[4,8,32,128]{3,2,1,0:T(8,128)S(1)}, u32[]{:S(2)}, u32[]{:S(2)}) %collective-permute-start.28) | collective-permute-done | bytes 524320 | tf_op jit(solution)/shard_map/ppermute | solution.py:453
  237.9 9.7 %density.7 = (f32[32,16,32,256]{3,2,1,0:T(8,128)}, f32[8,128]{1,0:T(8,128)}) custom-call(s32[5]{0:T(128)} %stack.29.info, f32[512]{0:T(512)} %reshape.12.price, f32[512]{0:T(512)} %reshape.13.rate, f32[32,16,32,256]{3,2,1,0:T(8,128)} %dens.9, f32[5,11,40,256]{3,2,1,0:T(8,128)} %copy-done, ...), custom_call_target="tpu_custom_call", output_to_operand_aliasing={{0}: (17, {})} | custom-call | flops 3221225472 | bytes 12582912 | tf_op jit(solution)/shard_map/density/pallas_call | solution.py:324
  249.9 19.4 %sweeps.9 = (f32[32,16,32,256]{3,2,1,0:T(8,128)}, f32[8,128]{1,0:T(8,128)}, f32[3,8,32,128]{3,2,1,0:T(8,128)}, f32[3,8,32,128]{3,2,1,0:T(8,128)}, f32[3,8,32,128...) custom-call(s32[5]{0:T(128)} %stack.29.info, ...), custom_call_target="tpu_custom_call", output_to_operand_aliasing={{0}: (9, {})} | custom-call | flops 7172259840 | bytes 9437184 | tf_op jit(solution)/shard_map/sweeps/pallas_call | solution.py:273
  271.3 12.0 %collective-permute-done.42.rest_5_ = f32[4,8,32,128]{3,2,1,0:T(8,128)S(1)} collective-permute-done((f32[4,8,32,128]{3,2,1,0:T(8,128)}, f32[4,8,32,128]{3,2,1,0:T(8,128)S(1)}, u32[]{:S(2)}, u32[]{:S(2)}) %collective-permute-start.42) | collective-permute-done | bytes 524320 | tf_op jit(solution)/shard_map/ppermute | solution.py:453
  284.1 2.1 collective-permute-start.35
  287.8 9.8 %density.8 = (f32[32,16,32,256]{3,2,1,0:T(8,128)}, f32[8,128]{1,0:T(8,128)}) custom-call(s32[5]{0:T(128)} %stack.29.info, f32[512]{0:T(512)} %reshape.12.price, f32[512]{0:T(512)} %reshape.13.rate, f32[32,16,32,256]{3,2,1,0:T(8,128)} %dens.9, f32[5,11,40,256]{3,2,1,0:T(8,128)} %copy-done, ...), custom_call_target="tpu_custom_call", output_to_operand_aliasing={{0}: (17, {})} | custom-call | flops 3221225472 | bytes 12582912 | tf_op jit(solution)/shard_map/density/pallas_call | solution.py:324
  297.6 22.2 %collective-permute-done.35.rest_5_ = f32[3,8,32,128]{3,2,1,0:T(8,128)} collective-permute-done((f32[3,8,32,128]{3,2,1,0:T(8,128)}, f32[3,8,32,128]{3,2,1,0:T(8,128)}, u32[]{:S(2)}, u32[]{:S(2)}) %collective-permute-start.35) | collective-permute-done | bytes 393248 | tf_op jit(solution)/shard_map/ppermute | solution.py:453
  319.8 8.0 %density.9 = (f32[32,16,32,256]{3,2,1,0:T(8,128)}, f32[8,128]{1,0:T(8,128)}) custom-call(s32[5]{0:T(128)} %stack.29.info, f32[512]{0:T(512)} %reshape.12.price, f32[512]{0:T(512)} %reshape.13.rate, f32[32,16,32,256]{3,2,1,0:T(8,128)} %dens.9, f32[5,11,40,256]{3,2,1,0:T(8,128)} %copy-done, ...), custom_call_target="tpu_custom_call", output_to_operand_aliasing={{0}: (17, {})} | custom-call | flops 2415919104 | bytes 9437184 | tf_op jit(solution)/shard_map/density/pallas_call | solution.py:324
  (187 shorter events, 68.6 us)
Async XLA Ops:
  5.8 27.7 %collective-permute-start.1 = (f32[40,5,4,256]{3,2,1,0:T(4,128)}, f32[40,5,4,256]{3,2,1,0:T(4,128)S(1)}, u32[]{:S(2)}, u32[]{:S(2)}) collective-permute-start(f32[40,5,4,256]{3,2,1,0:T(4,128)} %pad_maximum_fusion.3), channel_id=1, source_target_pairs={{0,1},{1,2},{2,3},{3,4},{4,5},{5,6},{6,7},{8,9},{9,10},{10,11},{11... | collective-permute-start | bytes 2457608 | tf_op jit(solution)/shard_map/ppermute | solution.py:349
  10.7 22.9 %collective-permute-start = (f32[40,5,4,256]{3,2,1,0:T(4,128)}, f32[40,5,4,256]{3,2,1,0:T(4,128)}, u32[]{:S(2)}, u32[]{:S(2)}) collective-permute-start(f32[40,5,4,256]{3,2,1,0:T(4,128)} %pad_maximum_fusion.2), channel_id=1, source_target_pairs={{1,0},{2,1},{3,2},{4,3},{5,4},{6,5},{7,6},{9,8},{10,9},{11,10},{12... | collective-permute-start | bytes 2457608 | tf_op jit(solution)/shard_map/ppermute | solution.py:350
  21.0 49.3 %collective-permute-start.6 = (f32[40,11,4,256]{3,2,1,0:T(4,128)}, f32[40,11,4,256]{3,2,1,0:T(4,128)S(1)}, u32[]{:S(2)}, u32[]{:S(2)}) collective-permute-start(f32[40,11,4,256]{3,2,1,0:T(4,128)} %pad_maximum_fusion.1), channel_id=1, source_target_pairs={{0,1},{1,2},{2,3},{3,4},{4,5},{5,6},{6,7},{8,9},{9,10},{10,11},{11... | collective-permute-start | bytes 5406728 | tf_op jit(solution)/shard_map/ppermute | solution.py:349
  26.6 43.7 %collective-permute-start.5 = (f32[40,11,4,256]{3,2,1,0:T(4,128)}, f32[40,11,4,256]{3,2,1,0:T(4,128)}, u32[]{:S(2)}, u32[]{:S(2)}) collective-permute-start(f32[40,11,4,256]{3,2,1,0:T(4,128)} %pad_maximum_fusion), channel_id=1, source_target_pairs={{1,0},{2,1},{3,2},{4,3},{5,4},{6,5},{7,6},{9,8},{10,9},{11,10},{12... | collective-permute-start | bytes 5406728 | tf_op jit(solution)/shard_map/ppermute | solution.py:350
  39.0 26.7 %collective-permute-start.2 = (f32[5,3,40,256]{3,2,1,0:T(8,128)}, f32[5,3,40,256]{3,2,1,0:T(8,128)}, u32[]{:S(2)}, u32[]{:S(2)}) collective-permute-start(f32[5,3,40,256]{3,2,1,0:T(8,128)} %select_maximum_fusion.5), channel_id=1, source_target_pairs={{0,8},{8,16},{16,24},{1,9},{9,17},{17,25},{2,10},{10,18},{18,26},{... | collective-permute-start | bytes 1843208 | tf_op jit(solution)/shard_map/ppermute | solution.py:349
  41.2 25.3 %collective-permute-start.3 = (f32[5,3,40,256]{3,2,1,0:T(8,128)}, f32[5,3,40,256]{3,2,1,0:T(8,128)}, u32[]{:S(2)}, u32[]{:S(2)}) collective-permute-start(f32[5,3,40,256]{3,2,1,0:T(8,128)} %fusion), channel_id=1, source_target_pairs={{8,0},{16,8},{24,16},{9,1},{17,9},{25,17},{10,2},{18,10},{26,18},{... | collective-permute-start | bytes 1843208 | tf_op jit(solution)/shard_map/ppermute | solution.py:350
  54.1 47.6 %collective-permute-start.9 = (f32[5,3,40,256]{3,2,1,0:T(8,128)}, f32[5,3,40,256]{3,2,1,0:T(8,128)S(1)}, u32[]{:S(2)}, u32[]{:S(2)}) collective-permute-start(f32[5,3,40,256]{3,2,1,0:T(8,128)} %select_maximum_fusion.2), channel_id=1, source_target_pairs={{8,0},{16,8},{24,16},{9,1},{17,9},{25,17},{10,2},{18,10},{26,18},{... | collective-permute-start | bytes 1843208 | tf_op jit(solution)/shard_map/ppermute | solution.py:350
  73.4 77.4 %collective-permute-start.7 = (f32[5,11,40,256]{3,2,1,0:T(8,128)}, f32[5,11,40,256]{3,2,1,0:T(8,128)S(1)}, u32[]{:S(2)}, u32[]{:S(2)}) collective-permute-start(f32[5,11,40,256]{3,2,1,0:T(8,128)} %select_maximum_fusion.1), channel_id=1, source_target_pairs={{0,8},{8,16},{16,24},{1,9},{9,17},{17,25},{2,10},{10,18},{18,26},{... | collective-permute-start | bytes 6758408 | tf_op jit(solution)/shard_map/ppermute | solution.py:349
  76.4 76.2 %collective-permute-start.8 = (f32[5,11,40,256]{3,2,1,0:T(8,128)}, f32[5,11,40,256]{3,2,1,0:T(8,128)}, u32[]{:S(2)}, u32[]{:S(2)}) collective-permute-start(f32[5,11,40,256]{3,2,1,0:T(8,128)} %select_maximum_fusion), channel_id=1, source_target_pairs={{8,0},{16,8},{24,16},{9,1},{17,9},{25,17},{10,2},{18,10},{26,18},{... | collective-permute-start | bytes 6758408 | tf_op jit(solution)/shard_map/ppermute | solution.py:350
  108.6 27.8 %collective-permute-start.14 = (f32[2,8,32,128]{3,2,1,0:T(8,128)}, f32[2,8,32,128]{3,2,1,0:T(8,128)S(1)}, u32[]{:S(2)}, u32[]{:S(2)}) collective-permute-start(f32[2,8,32,128]{3,2,1,0:T(8,128)} %get-tuple-element.66), channel_id=1, source_target_pairs={{0,5},{1,4},{2,7},{3,6},{4,1},{5,0},{6,3},{7,2},{8,13},{9,12},{10,... | collective-permute-start | bytes 786440 | tf_op jit(solution)/shard_map/ppermute | solution.py:453
  114.4 22.2 %collective-permute-start.15 = (f32[2,8,32,128]{3,2,1,0:T(8,128)}, f32[2,8,32,128]{3,2,1,0:T(8,128)S(1)}, u32[]{:S(2)}, u32[]{:S(2)}) collective-permute-start(f32[2,8,32,128]{3,2,1,0:T(8,128)} %get-tuple-element.67), channel_id=1, source_target_pairs={{0,6},{1,7},{2,4},{3,5},{4,2},{5,3},{6,0},{7,1},{8,14},{9,15},{10,... | collective-permute-start | bytes 786440 | tf_op jit(solution)/shard_map/ppermute | solution.py:453
  116.1 26.1 %collective-permute-start.16 = (f32[2,8,32,128]{3,2,1,0:T(8,128)}, f32[2,8,32,128]{3,2,1,0:T(8,128)}, u32[]{:S(2)}, u32[]{:S(2)}) collective-permute-start(f32[2,8,32,128]{3,2,1,0:T(8,128)} %get-tuple-element.68), channel_id=1, source_target_pairs={{0,7},{1,6},{2,5},{3,4},{4,3},{5,2},{6,1},{7,0},{8,15},{9,14},{10,... | collective-permute-start | bytes 786440 | tf_op jit(solution)/shard_map/ppermute | solution.py:453
  142.2 36.0 %collective-permute-start.19 = (f32[3,8,32,128]{3,2,1,0:T(8,128)}, f32[3,8,32,128]{3,2,1,0:T(8,128)S(1)}, u32[]{:S(2)}, u32[]{:S(2)}) collective-permute-start(f32[3,8,32,128]{3,2,1,0:T(8,128)} %get-tuple-element.75), channel_id=1, source_target_pairs={{0,3},{1,2},{2,1},{3,0},{4,7},{5,6},{6,5},{7,4},{8,11},{9,10},{10,... | collective-permute-start | bytes 1179656 | tf_op jit(solution)/shard_map/ppermute | solution.py:453
  149.0 29.6 %collective-permute-start.20 = (f32[3,8,32,128]{3,2,1,0:T(8,128)}, f32[3,8,32,128]{3,2,1,0:T(8,128)S(1)}, u32[]{:S(2)}, u32[]{:S(2)}) collective-permute-start(f32[3,8,32,128]{3,2,1,0:T(8,128)} %get-tuple-element.76), channel_id=1, source_target_pairs={{0,4},{1,5},{2,6},{3,7},{4,0},{5,1},{6,2},{7,3},{8,12},{9,13},{10,... | collective-permute-start | bytes 1179656 | tf_op jit(solution)/shard_map/ppermute | solution.py:453
  149.6 36.1 %collective-permute-start.21 = (f32[3,8,32,128]{3,2,1,0:T(8,128)}, f32[3,8,32,128]{3,2,1,0:T(8,128)}, u32[]{:S(2)}, u32[]{:S(2)}) collective-permute-start(f32[3,8,32,128]{3,2,1,0:T(8,128)} %get-tuple-element.77), channel_id=1, source_target_pairs={{0,5},{1,4},{2,7},{3,6},{4,1},{5,0},{6,3},{7,2},{8,13},{9,12},{10,... | collective-permute-start | bytes 1179656 | tf_op jit(solution)/shard_map/ppermute | solution.py:453
  150.8 36.2 %collective-permute-start.22 = (f32[3,8,32,128]{3,2,1,0:T(8,128)}, f32[3,8,32,128]{3,2,1,0:T(8,128)}, u32[]{:S(2)}, u32[]{:S(2)}) collective-permute-start(f32[3,8,32,128]{3,2,1,0:T(8,128)} %get-tuple-element.78), channel_id=1, source_target_pairs={{0,6},{1,7},{2,4},{3,5},{4,2},{5,3},{6,0},{7,1},{8,14},{9,15},{10,... | collective-permute-start | bytes 1179656 | tf_op jit(solution)/shard_map/ppermute | solution.py:453
  152.5 34.9 %collective-permute-start.23 = (f32[3,8,32,128]{3,2,1,0:T(8,128)}, f32[3,8,32,128]{3,2,1,0:T(8,128)}, u32[]{:S(2)}, u32[]{:S(2)}) collective-permute-start(f32[3,8,32,128]{3,2,1,0:T(8,128)} %get-tuple-element.79), channel_id=1, source_target_pairs={{0,7},{1,6},{2,5},{3,4},{4,3},{5,2},{6,1},{7,0},{8,15},{9,14},{10,... | collective-permute-start | bytes 1179656 | tf_op jit(solution)/shard_map/ppermute | solution.py:453
  185.7 38.9 %collective-permute-start.26 = (f32[4,8,32,128]{3,2,1,0:T(8,128)}, f32[4,8,32,128]{3,2,1,0:T(8,128)S(1)}, u32[]{:S(2)}, u32[]{:S(2)}) collective-permute-start(f32[4,8,32,128]{3,2,1,0:T(8,128)} %get-tuple-element.87), channel_id=1, source_target_pairs={{0,3},{1,2},{2,1},{3,0},{4,7},{5,6},{6,5},{7,4},{8,11},{9,10},{10,... | collective-permute-start | bytes 1572872 | tf_op jit(solution)/shard_map/ppermute | solution.py:453
  187.0 38.4 %collective-permute-start.27 = (f32[4,8,32,128]{3,2,1,0:T(8,128)}, f32[4,8,32,128]{3,2,1,0:T(8,128)S(1)}, u32[]{:S(2)}, u32[]{:S(2)}) collective-permute-start(f32[4,8,32,128]{3,2,1,0:T(8,128)} %get-tuple-element.88), channel_id=1, source_target_pairs={{0,4},{1,5},{2,6},{3,7},{4,0},{5,1},{6,2},{7,3},{8,12},{9,13},{10,... | collective-permute-start | bytes 1572872 | tf_op jit(solution)/shard_map/ppermute | solution.py:453
  187.4 47.5 %collective-permute-start.28 = (f32[4,8,32,128]{3,2,1,0:T(8,128)}, f32[4,8,32,128]{3,2,1,0:T(8,128)S(1)}, u32[]{:S(2)}, u32[]{:S(2)}) collective-permute-start(f32[4,8,32,128]{3,2,1,0:T(8,128)} %get-tuple-element.89), channel_id=1, source_target_pairs={{0,5},{1,4},{2,7},{3,6},{4,1},{5,0},{6,3},{7,2},{8,13},{9,12},{10,... | collective-permute-start | bytes 1572872 | tf_op jit(solution)/shard_map/ppermute | solution.py:453
  197.1 38.6 %collective-permute-start.29 = (f32[4,8,32,128]{3,2,1,0:T(8,128)}, f32[4,8,32,128]{3,2,1,0:T(8,128)}, u32[]{:S(2)}, u32[]{:S(2)}) collective-permute-start(f32[4,8,32,128]{3,2,1,0:T(8,128)} %get-tuple-element.90), channel_id=1, source_target_pairs={{0,6},{1,7},{2,4},{3,5},{4,2},{5,3},{6,0},{7,1},{8,14},{9,15},{10,... | collective-permute-start | bytes 1572872 | tf_op jit(solution)/shard_map/ppermute | solution.py:453
  197.5 38.6 %collective-permute-start.30 = (f32[4,8,32,128]{3,2,1,0:T(8,128)}, f32[4,8,32,128]{3,2,1,0:T(8,128)}, u32[]{:S(2)}, u32[]{:S(2)}) collective-permute-start(f32[4,8,32,128]{3,2,1,0:T(8,128)} %get-tuple-element.91), channel_id=1, source_target_pairs={{0,7},{1,6},{2,5},{3,4},{4,3},{5,2},{6,1},{7,0},{8,15},{9,14},{10,... | collective-permute-start | bytes 1572872 | tf_op jit(solution)/shard_map/ppermute | solution.py:453
  224.7 23.0 %collective-permute-start.38 = (f32[4,8,32,128]{3,2,1,0:T(8,128)}, f32[4,8,32,128]{3,2,1,0:T(8,128)S(1)}, u32[]{:S(2)}, u32[]{:S(2)}) collective-permute-start(f32[4,8,32,128]{3,2,1,0:T(8,128)} %get-tuple-element.105), channel_id=1, source_target_pairs={{0,1},{1,0},{2,3},{3,2},{4,5},{5,4},{6,7},{7,6},{8,9},{9,8},{10,11... | collective-permute-start | bytes 1572872 | tf_op jit(solution)/shard_map/ppermute | solution.py:453
  225.4 23.7 %collective-permute-start.39 = (f32[4,8,32,128]{3,2,1,0:T(8,128)}, f32[4,8,32,128]{3,2,1,0:T(8,128)S(1)}, u32[]{:S(2)}, u32[]{:S(2)}) collective-permute-start(f32[4,8,32,128]{3,2,1,0:T(8,128)} %get-tuple-element.106), channel_id=1, source_target_pairs={{0,2},{1,3},{2,0},{3,1},{4,6},{5,7},{6,4},{7,5},{8,10},{9,11},{10,... | collective-permute-start | bytes 1572872 | tf_op jit(solution)/shard_map/ppermute | solution.py:453
  235.7 33.6 %collective-permute-start.40 = (f32[4,8,32,128]{3,2,1,0:T(8,128)}, f32[4,8,32,128]{3,2,1,0:T(8,128)S(1)}, u32[]{:S(2)}, u32[]{:S(2)}) collective-permute-start(f32[4,8,32,128]{3,2,1,0:T(8,128)} %get-tuple-element.107), channel_id=1, source_target_pairs={{0,3},{1,2},{2,1},{3,0},{4,7},{5,6},{6,5},{7,4},{8,11},{9,10},{10,... | collective-permute-start | bytes 1572872 | tf_op jit(solution)/shard_map/ppermute | solution.py:453
  235.7 34.4 %collective-permute-start.41 = (f32[4,8,32,128]{3,2,1,0:T(8,128)}, f32[4,8,32,128]{3,2,1,0:T(8,128)S(1)}, u32[]{:S(2)}, u32[]{:S(2)}) collective-permute-start(f32[4,8,32,128]{3,2,1,0:T(8,128)} %get-tuple-element.108), channel_id=1, source_target_pairs={{0,4},{1,5},{2,6},{3,7},{4,0},{5,1},{6,2},{7,3},{8,12},{9,13},{10,... | collective-permute-start | bytes 1572872 | tf_op jit(solution)/shard_map/ppermute | solution.py:453
  236.1 47.2 %collective-permute-start.42 = (f32[4,8,32,128]{3,2,1,0:T(8,128)}, f32[4,8,32,128]{3,2,1,0:T(8,128)S(1)}, u32[]{:S(2)}, u32[]{:S(2)}) collective-permute-start(f32[4,8,32,128]{3,2,1,0:T(8,128)} %get-tuple-element.109), channel_id=1, source_target_pairs={{0,5},{1,4},{2,7},{3,6},{4,1},{5,0},{6,3},{7,2},{8,13},{9,12},{10,... | collective-permute-start | bytes 1572872 | tf_op jit(solution)/shard_map/ppermute | solution.py:453
  247.6 35.6 %collective-permute-start.43 = (f32[4,8,32,128]{3,2,1,0:T(8,128)}, f32[4,8,32,128]{3,2,1,0:T(8,128)S(1)}, u32[]{:S(2)}, u32[]{:S(2)}) collective-permute-start(f32[4,8,32,128]{3,2,1,0:T(8,128)} %get-tuple-element.110), channel_id=1, source_target_pairs={{0,6},{1,7},{2,4},{3,5},{4,2},{5,3},{6,0},{7,1},{8,14},{9,15},{10,... | collective-permute-start | bytes 1572872 | tf_op jit(solution)/shard_map/ppermute | solution.py:453
  249.1 35.0 %collective-permute-start.44 = (f32[4,8,32,128]{3,2,1,0:T(8,128)}, f32[4,8,32,128]{3,2,1,0:T(8,128)S(1)}, u32[]{:S(2)}, u32[]{:S(2)}) collective-permute-start(f32[4,8,32,128]{3,2,1,0:T(8,128)} %get-tuple-element.111), channel_id=1, source_target_pairs={{0,7},{1,6},{2,5},{3,4},{4,3},{5,2},{6,1},{7,0},{8,15},{9,14},{10,... | collective-permute-start | bytes 1572872 | tf_op jit(solution)/shard_map/ppermute | solution.py:453
  284.1 35.7 %collective-permute-start.35 = (f32[3,8,32,128]{3,2,1,0:T(8,128)}, f32[3,8,32,128]{3,2,1,0:T(8,128)}, u32[]{:S(2)}, u32[]{:S(2)}) collective-permute-start(f32[3,8,32,128]{3,2,1,0:T(8,128)} %get-tuple-element.101), channel_id=1, source_target_pairs={{0,5},{1,4},{2,7},{3,6},{4,1},{5,0},{6,3},{7,2},{8,13},{9,12},{10,... | collective-permute-start | bytes 1179656 | tf_op jit(solution)/shard_map/ppermute | solution.py:453
  286.2 33.6 %collective-permute-start.36 = (f32[3,8,32,128]{3,2,1,0:T(8,128)}, f32[3,8,32,128]{3,2,1,0:T(8,128)}, u32[]{:S(2)}, u32[]{:S(2)}) collective-permute-start(f32[3,8,32,128]{3,2,1,0:T(8,128)} %get-tuple-element.102), channel_id=1, source_target_pairs={{0,6},{1,7},{2,4},{3,5},{4,2},{5,3},{6,0},{7,1},{8,14},{9,15},{10,... | collective-permute-start | bytes 1179656 | tf_op jit(solution)/shard_map/ppermute | solution.py:453
  286.9 32.9 %collective-permute-start.37 = (f32[3,8,32,128]{3,2,1,0:T(8,128)}, f32[3,8,32,128]{3,2,1,0:T(8,128)}, u32[]{:S(2)}, u32[]{:S(2)}) collective-permute-start(f32[3,8,32,128]{3,2,1,0:T(8,128)} %get-tuple-element.103), channel_id=1, source_target_pairs={{0,7},{1,6},{2,5},{3,4},{4,3},{5,2},{6,1},{7,0},{8,15},{9,14},{10,... | collective-permute-start | bytes 1179656 | tf_op jit(solution)/shard_map/ppermute | solution.py:453
  (44 other events, 557.1 us)
where the time goes:
time: 335 us; the launch traced here: 328 us
  Pallas kernels  144 us (43%)
  waiting for transfers between devices  68.8 us (21%)
  starting transfers between devices  63.2 us (19%)
  local copies, waits for them, and re-layouts  33.4 us (10%)
  other arithmetic  17.4 us (5%)
    pallas_call x5, Pallas kernels, run_sweeps(): pl.pallas_call(functools.partial(sweep_kernel, first, n, extra), grid=(si...  102 us
    ppermute x35, waiting for transfers between devices, on_device(): lax.ppermute(sends[d], 'state', [(i, i ^ d) for i in range(n)])  59.9 us
    pallas_call x5, Pallas kernels, run_density(): pl.pallas_call(functools.partial(density_kernel, first, n, extra), grid=(...  41.7 us
    ppermute x35, starting transfers between devices, on_device(): lax.ppermute(sends[d], 'state', [(i, i ^ d) for i in range(n)])  35.2 us
    ppermute x5, starting transfers between devices, neighbours(): after = lax.ppermute(head, axis, [(i + 1, i) for i in range(ends)])  16.9 us
    ppermute x5, starting transfers between devices, neighbours(): before = lax.ppermute(tail, axis, [(i, i + 1) for i in range(ends)])  11.1 us
    ppermute x5, waiting for transfers between devices, neighbours(): before = lax.ppermute(tail, axis, [(i, i + 1) for i in range(ends)])  8.81 us
  transfers between devices with their start and end apart: 45, of which 8 were waited for; matrix products, arithmetic and copies ran while one was open for 13% of the time, Pallas kernels for 41%

commit v1 on v0

--- a/solution.py
+++ b/solution.py
@@ -76,7 +76,7 @@
 
     @pl.when(step == 0)
     def _():
-        high, low = split_parts(tank[...])
+        high, low = split_parts(tank[...].T)
         t_high[...] = high
         t_low[...] = low
 
@@ -178,7 +178,7 @@
 
     @pl.when(step == 0)
     def _():
-        m = soc[...]
+        m = soc[...].T
         high, low = split_parts(m)
         m_high[...] = high
         m_low[...] = low
@@ -406,7 +406,7 @@
     pair = jnp.stack([price, wind_rate], axis=1)
     slot = jnp.pad(pair[:, None], ((0, 0), (0, 0), (0, rows + 2 * HALO - 2), (0, cols - rooms)))
     price_flat, rate_flat = price.reshape(-1), wind_rate.reshape(-1)
-    tank, soc = tank_inverse.T, soc_inverse.T
+    tank, soc = tank_inverse, soc_inverse
 
     sweep_done, density_done, takes = {}, {}, {}
     value, density_next = None, None
@@ -425,7 +425,7 @@
     wide = jnp.concatenate([wl[:HALO, sizes[0], :2, :rooms], pair, wr[:HALO, sizes[0], :2, :rooms]], axis=0)
     price_wide, rate_wide = wide[:, 0].reshape(-1), wide[:, 1].reshape(-1)
     second_winds = winds(sizes[0], sizes[1], first_sides, sizes[0], None)
-    later_winds = winds(early, later, later_sides, 0, 0.0 * second_winds[0][0, 0])
+    later_winds = winds(early, later, later_sides, 0, 0.0 * first_winds[0][0, 0])
 
     def halos_of(c):
         if c == 0:

time: 335 us -> 327 us (0.976)
  local copies, waits for them, and re-layouts: 33.4 us -> 27.4 us
    ppermute x5, waiting for transfers between devices: 0.01 us -> 4.7 us  [neighbours(): after = lax.ppermute(head, axis, [(i + 1, i) for i in range(ends)])]
    unnamed x70 -> x76, local copies, waits for them, and re-layouts: 6.05 us -> 1.73 us
  transfers between devices with their start and end apart: 45 -> 45, of which waited for: 8 -> 8; matrix products, arithmetic and copies ran while one was open for 13% -> 11% of each run, Pallas kernels for 41% -> 43%
where the time goes in v1:
time: 327 us; the launch traced here: 321 us
  Pallas kernels  145 us (44%)
  waiting for transfers between devices  69.3 us (21%)
  starting transfers between devices  62.8 us (19%)
  local copies, waits for them, and re-layouts  27.4 us (8%)
  other arithmetic  15.1 us (5%)
    pallas_call x5, Pallas kernels, run_sweeps(): pl.pallas_call(functools.partial(sweep_kernel, first, n, extra), grid=(si...  103 us
    ppermute x35, waiting for transfers between devices, on_device(): lax.ppermute(sends[d], 'state', [(i, i ^ d) for i in range(n)])  57.6 us
    pallas_call x5, Pallas kernels, run_density(): pl.pallas_call(functools.partial(density_kernel, first, n, extra), grid=(...  42.1 us
    ppermute x35, starting transfers between devices, on_device(): lax.ppermute(sends[d], 'state', [(i, i ^ d) for i in range(n)])  34.6 us
    ppermute x5, starting transfers between devices, neighbours(): after = lax.ppermute(head, axis, [(i + 1, i) for i in range(ends)])  17 us
    ppermute x5, starting transfers between devices, neighbours(): before = lax.ppermute(tail, axis, [(i, i + 1) for i in range(ends)])  11.1 us
    ppermute x5, waiting for transfers between devices, neighbours(): before = lax.ppermute(tail, axis, [(i, i + 1) for i in range(ends)])  6.94 us
  transfers between devices with their start and end apart: 45, of which 8 were waited for; matrix products, arithmetic and copies ran while one was open for 11% of the time, Pallas kernels for 43%

profile of v1, /device:TPU:25, one launch (start us, length us, event | category | flops | bytes accessed | tf_op | source)
XLA Modules:
  0.0 320.8 jit_solution(7996038266664877701)
XLA Ops:
  0.6 2.0 fusion.13
  2.7 2.0 fusion.12
  5.8 3.7 %collective-permute-start.1 = (f32[40,5,4,256]{3,2,1,0:T(4,128)}, f32[40,5,4,256]{3,2,1,0:T(4,128)S(1)}, u32[]{:S(2)}, u32[]{:S(2)}) collective-permute-start(f32[40,5,4,256]{3,2,1,0:T(4,128)} %pad_maximum_fusion.3), channel_id=1, source_target_pairs={{0,1},{1,2},{2,3},{3,4},{4,5},{5,6},{6,7},{8,9},{9,10},{10,11},{11... | collective-permute-start | bytes 2457608 | tf_op jit(solution)/shard_map/ppermute | solution.py:349
  12.6 3.2 %fusion.9 = (f32[32,11,1,256]{3,2,1,0:T(1,128)S(1)}, f32[32,11,1,256]{3,2,1,0:T(1,128)S(1)}) fusion(f32[32,16,32,256]{3,2,1,0:T(8,128)} %dens.9), kind=kLoop, calls=%fused_computation.37 | loop fusion | bytes 1441792 | tf_op jit(solution)/shard_map/slice | solution.py:366
  15.8 3.2 %fusion.8 = (f32[32,11,4,256]{3,2,1,0:T(4,128)S(1)}, f32[32,11,4,256]{3,2,1,0:T(4,128)S(1)}) fusion(f32[32,16,32,256]{3,2,1,0:T(8,128)} %v.9), kind=kLoop, calls=%fused_computation.36 | loop fusion | bytes 5767168 | tf_op jit(solution)/shard_map/slice | solution.py:366
  21.0 3.6 %collective-permute-start.5 = (f32[40,11,4,256]{3,2,1,0:T(4,128)}, f32[40,11,4,256]{3,2,1,0:T(4,128)S(1)}, u32[]{:S(2)}, u32[]{:S(2)}) collective-permute-start(f32[40,11,4,256]{3,2,1,0:T(4,128)} %pad_maximum_fusion.1), channel_id=1, source_target_pairs={{0,1},{1,2},{2,3},{3,4},{4,5},{5,6},{6,7},{8,9},{9,10},{10,11},{11... | collective-permute-start | bytes 5406728 | tf_op jit(solution)/shard_map/ppermute | solution.py:349
  33.8 2.1 fusion.7
  40.3 4.8 %collective-permute-start.3 = (f32[5,3,40,256]{3,2,1,0:T(8,128)}, f32[5,3,40,256]{3,2,1,0:T(8,128)}, u32[]{:S(2)}, u32[]{:S(2)}) collective-permute-start(f32[5,3,40,256]{3,2,1,0:T(8,128)} %fusion), channel_id=1, source_target_pairs={{8,0},{16,8},{24,16},{9,1},{17,9},{25,17},{10,2},{18,10},{26,18},{... | collective-permute-start | bytes 1843208 | tf_op jit(solution)/shard_map/ppermute | solution.py:350
  49.1 6.9 %collective-permute-done.2.wl = f32[5,3,40,256]{3,2,1,0:T(8,128)S(1)} collective-permute-done((f32[5,3,40,256]{3,2,1,0:T(8,128)S(1)}, f32[5,3,40,256]{3,2,1,0:T(8,128)S(1)}, u32[]{:S(2)}, u32[]{:S(2)}) %collective-permute-start.2) | collective-permute-done | bytes 614432 | tf_op jit(solution)/shard_map/ppermute | solution.py:349
  56.0 2.9 collective-permute-start.9
  60.5 2.9 slice_add_fusion
  63.4 4.7 %collective-permute-done.4.sr.kr = f32[40,11,4,256]{3,2,1,0:T(4,128)} collective-permute-done((f32[40,11,4,256]{3,2,1,0:T(4,128)}, f32[40,11,4,256]{3,2,1,0:T(4,128)}, u32[]{:S(2)}, u32[]{:S(2)}) %collective-permute-start.4) | collective-permute-done | bytes 1802272 | tf_op jit(solution)/shard_map/ppermute | solution.py:350
  73.7 5.5 %collective-permute-start.7 = (f32[5,11,40,256]{3,2,1,0:T(8,128)}, f32[5,11,40,256]{3,2,1,0:T(8,128)}, u32[]{:S(2)}, u32[]{:S(2)}) collective-permute-start(f32[5,11,40,256]{3,2,1,0:T(8,128)} %select_maximum_fusion), channel_id=1, source_target_pairs={{8,0},{16,8},{24,16},{9,1},{17,9},{25,17},{10,2},{18,10},{26,18},{... | collective-permute-start | bytes 6758408 | tf_op jit(solution)/shard_map/ppermute | solution.py:350
  80.7 13.8 %sweeps.5 = (f32[32,16,32,256]{3,2,1,0:T(8,128)}, f32[8,128]{1,0:T(8,128)}, f32[2,8,32,128]{3,2,1,0:T(8,128)}, f32[2,8,32,128]{3,2,1,0:T(8,128)}, f32[2,8,32,128...) custom-call(s32[5]{0:T(128)} %stack.29.info, ...), custom_call_target="tpu_custom_call" | custom-call | flops 4781506560 | bytes 6291456 | tf_op jit(solution)/shard_map/sweeps/pallas_call | solution.py:273
  97.3 5.1 %collective-permute-done.11.rest_2_ = f32[2,8,32,128]{3,2,1,0:T(8,128)S(1)} collective-permute-done((f32[2,8,32,128]{3,2,1,0:T(8,128)}, f32[2,8,32,128]{3,2,1,0:T(8,128)S(1)}, u32[]{:S(2)}, u32[]{:S(2)}) %collective-permute-start.11) | collective-permute-done | bytes 262176 | tf_op jit(solution)/shard_map/ppermute | solution.py:453
  102.4 2.5 collective-permute-start.14
  104.9 3.9 %collective-permute-done.12.rest_3_ = f32[2,8,32,128]{3,2,1,0:T(8,128)} collective-permute-done((f32[2,8,32,128]{3,2,1,0:T(8,128)}, f32[2,8,32,128]{3,2,1,0:T(8,128)}, u32[]{:S(2)}, u32[]{:S(2)}) %collective-permute-start.12) | collective-permute-done | bytes 262176 | tf_op jit(solution)/shard_map/ppermute | solution.py:453
  110.9 19.3 %sweeps.6 = (f32[32,16,32,256]{3,2,1,0:T(8,128)}, f32[8,128]{1,0:T(8,128)}, f32[3,8,32,128]{3,2,1,0:T(8,128)}, f32[3,8,32,128]{3,2,1,0:T(8,128)}, f32[3,8,32,128...) custom-call(s32[5]{0:T(128)} %stack.29.info, ...), custom_call_target="tpu_custom_call", output_to_operand_aliasing={{0}: (9, {})} | custom-call | flops 7172259840 | bytes 9437184 | tf_op jit(solution)/shard_map/sweeps/pallas_call | solution.py:273
  135.3 6.3 %density.5 = (f32[32,16,32,256]{3,2,1,0:T(8,128)}, f32[8,128]{1,0:T(8,128)}) custom-call(s32[5]{0:T(128)} %stack.29.info, f32[512]{0:T(512)} %reshape.12.price, f32[512]{0:T(512)} %reshape.13.rate, f32[32,16,32,256]{3,2,1,0:T(8,128)} %dens.9, f32[5,3,40,256]{3,2,1,0:T(8,128)} %copy-done.3, f32[5,3,40,256]{3,2,1,0:T(8,128)} %collective-permute-done.3.wr, ...), custom_call_target="tpu_custom_call" | custom-call | flops 1610612736 | bytes 6291456 | tf_op jit(solution)/shard_map/density/pallas_call | solution.py:324
  142.6 2.6 collective-permute-start.21
  147.2 24.8 %sweeps.7 = (f32[32,16,32,256]{3,2,1,0:T(8,128)}, f32[8,128]{1,0:T(8,128)}, f32[4,8,32,128]{3,2,1,0:T(8,128)}, f32[4,8,32,128]{3,2,1,0:T(8,128)}, f32[4,8,32,128...) custom-call(s32[5]{0:T(128)} %stack.29.info, ...), custom_call_target="tpu_custom_call", output_to_operand_aliasing={{0}: (9, {})} | custom-call | flops 9563013120 | bytes 12582912 | tf_op jit(solution)/shard_map/sweeps/pallas_call | solution.py:273
  173.3 5.1 %collective-permute-done.21.rest_5_ = f32[3,8,32,128]{3,2,1,0:T(8,128)} collective-permute-done((f32[3,8,32,128]{3,2,1,0:T(8,128)}, f32[3,8,32,128]{3,2,1,0:T(8,128)}, u32[]{:S(2)}, u32[]{:S(2)}) %collective-permute-start.21) | collective-permute-done | bytes 393248 | tf_op jit(solution)/shard_map/ppermute | solution.py:453
  181.5 8.0 %density.6 = (f32[32,16,32,256]{3,2,1,0:T(8,128)}, f32[8,128]{1,0:T(8,128)}) custom-call(s32[5]{0:T(128)} %stack.29.info, f32[512]{0:T(512)} %reshape.12.price, f32[512]{0:T(512)} %reshape.13.rate, f32[32,16,32,256]{3,2,1,0:T(8,128)} %dens.9, f32[5,3,40,256]{3,2,1,0:T(8,128)} %collective-permute-done.8.wl, ...), custom_call_target="tpu_custom_call", output_to_operand_aliasing={{0}: (17, {})} | custom-call | flops 2415919104 | bytes 9437184 | tf_op jit(solution)/shard_map/density/pallas_call | solution.py:324
  192.4 25.2 %sweeps.8 = (f32[32,16,32,256]{3,2,1,0:T(8,128)}, f32[8,128]{1,0:T(8,128)}, f32[4,8,32,128]{3,2,1,0:T(8,128)}, f32[4,8,32,128]{3,2,1,0:T(8,128)}, f32[4,8,32,128...) custom-call(s32[5]{0:T(128)} %stack.29.info, ...), custom_call_target="tpu_custom_call", output_to_operand_aliasing={{0}: (9, {})} | custom-call | flops 9563013120 | bytes 12582912 | tf_op jit(solution)/shard_map/sweeps/pallas_call | solution.py:273
  218.1 9.5 %collective-permute-done.28.rest_5_ = f32[4,8,32,128]{3,2,1,0:T(8,128)S(1)} collective-permute-done((f32[4,8,32,128]{3,2,1,0:T(8,128)}, f32[4,8,32,128]{3,2,1,0:T(8,128)S(1)}, u32[]{:S(2)}, u32[]{:S(2)}) %collective-permute-start.28) | collective-permute-done | bytes 524320 | tf_op jit(solution)/shard_map/ppermute | solution.py:453
  230.0 9.8 %density.7 = (f32[32,16,32,256]{3,2,1,0:T(8,128)}, f32[8,128]{1,0:T(8,128)}) custom-call(s32[5]{0:T(128)} %stack.29.info, f32[512]{0:T(512)} %reshape.12.price, f32[512]{0:T(512)} %reshape.13.rate, f32[32,16,32,256]{3,2,1,0:T(8,128)} %dens.9, f32[5,11,40,256]{3,2,1,0:T(8,128)} %copy-done, ...), custom_call_target="tpu_custom_call", output_to_operand_aliasing={{0}: (17, {})} | custom-call | flops 3221225472 | bytes 12582912 | tf_op jit(solution)/shard_map/density/pallas_call | solution.py:324
  242.0 19.5 %sweeps.9 = (f32[32,16,32,256]{3,2,1,0:T(8,128)}, f32[8,128]{1,0:T(8,128)}, f32[3,8,32,128]{3,2,1,0:T(8,128)}, f32[3,8,32,128]{3,2,1,0:T(8,128)}, f32[3,8,32,128...) custom-call(s32[5]{0:T(128)} %stack.29.info, ...), custom_call_target="tpu_custom_call", output_to_operand_aliasing={{0}: (9, {})} | custom-call | flops 7172259840 | bytes 9437184 | tf_op jit(solution)/shard_map/sweeps/pallas_call | solution.py:273
  263.5 11.9 %collective-permute-done.42.rest_5_ = f32[4,8,32,128]{3,2,1,0:T(8,128)S(1)} collective-permute-done((f32[4,8,32,128]{3,2,1,0:T(8,128)}, f32[4,8,32,128]{3,2,1,0:T(8,128)S(1)}, u32[]{:S(2)}, u32[]{:S(2)}) %collective-permute-start.42) | collective-permute-done | bytes 524320 | tf_op jit(solution)/shard_map/ppermute | solution.py:453
  276.5 2.1 collective-permute-start.35
  280.5 9.8 %density.8 = (f32[32,16,32,256]{3,2,1,0:T(8,128)}, f32[8,128]{1,0:T(8,128)}) custom-call(s32[5]{0:T(128)} %stack.29.info, f32[512]{0:T(512)} %reshape.12.price, f32[512]{0:T(512)} %reshape.13.rate, f32[32,16,32,256]{3,2,1,0:T(8,128)} %dens.9, f32[5,11,40,256]{3,2,1,0:T(8,128)} %copy-done, ...), custom_call_target="tpu_custom_call", output_to_operand_aliasing={{0}: (17, {})} | custom-call | flops 3221225472 | bytes 12582912 | tf_op jit(solution)/shard_map/density/pallas_call | solution.py:324
  290.4 22.1 %collective-permute-done.35.rest_5_ = f32[3,8,32,128]{3,2,1,0:T(8,128)} collective-permute-done((f32[3,8,32,128]{3,2,1,0:T(8,128)}, f32[3,8,32,128]{3,2,1,0:T(8,128)}, u32[]{:S(2)}, u32[]{:S(2)}) %collective-permute-start.35) | collective-permute-done | bytes 393248 | tf_op jit(solution)/shard_map/ppermute | solution.py:453
  312.5 8.1 %density.9 = (f32[32,16,32,256]{3,2,1,0:T(8,128)}, f32[8,128]{1,0:T(8,128)}) custom-call(s32[5]{0:T(128)} %stack.29.info, f32[512]{0:T(512)} %reshape.12.price, f32[512]{0:T(512)} %reshape.13.rate, f32[32,16,32,256]{3,2,1,0:T(8,128)} %dens.9, f32[5,11,40,256]{3,2,1,0:T(8,128)} %copy-done, ...), custom_call_target="tpu_custom_call", output_to_operand_aliasing={{0}: (17, {})} | custom-call | flops 2415919104 | bytes 9437184 | tf_op jit(solution)/shard_map/density/pallas_call | solution.py:324
  (193 shorter events, 62.3 us)
Async XLA Ops:
  5.8 31.4 %collective-permute-start.1 = (f32[40,5,4,256]{3,2,1,0:T(4,128)}, f32[40,5,4,256]{3,2,1,0:T(4,128)S(1)}, u32[]{:S(2)}, u32[]{:S(2)}) collective-permute-start(f32[40,5,4,256]{3,2,1,0:T(4,128)} %pad_maximum_fusion.3), channel_id=1, source_target_pairs={{0,1},{1,2},{2,3},{3,4},{4,5},{5,6},{6,7},{8,9},{9,10},{10,11},{11... | collective-permute-start | bytes 2457608 | tf_op jit(solution)/shard_map/ppermute | solution.py:349
  10.7 26.5 %collective-permute-start = (f32[40,5,4,256]{3,2,1,0:T(4,128)}, f32[40,5,4,256]{3,2,1,0:T(4,128)}, u32[]{:S(2)}, u32[]{:S(2)}) collective-permute-start(f32[40,5,4,256]{3,2,1,0:T(4,128)} %pad_maximum_fusion.2), channel_id=1, source_target_pairs={{1,0},{2,1},{3,2},{4,3},{5,4},{6,5},{7,6},{9,8},{10,9},{11,10},{12... | collective-permute-start | bytes 2457608 | tf_op jit(solution)/shard_map/ppermute | solution.py:350
  21.0 42.4 %collective-permute-start.5 = (f32[40,11,4,256]{3,2,1,0:T(4,128)}, f32[40,11,4,256]{3,2,1,0:T(4,128)S(1)}, u32[]{:S(2)}, u32[]{:S(2)}) collective-permute-start(f32[40,11,4,256]{3,2,1,0:T(4,128)} %pad_maximum_fusion.1), channel_id=1, source_target_pairs={{0,1},{1,2},{2,3},{3,4},{4,5},{5,6},{6,7},{8,9},{9,10},{10,11},{11... | collective-permute-start | bytes 5406728 | tf_op jit(solution)/shard_map/ppermute | solution.py:349
  26.6 41.5 %collective-permute-start.4 = (f32[40,11,4,256]{3,2,1,0:T(4,128)}, f32[40,11,4,256]{3,2,1,0:T(4,128)}, u32[]{:S(2)}, u32[]{:S(2)}) collective-permute-start(f32[40,11,4,256]{3,2,1,0:T(4,128)} %pad_maximum_fusion), channel_id=1, source_target_pairs={{1,0},{2,1},{3,2},{4,3},{5,4},{6,5},{7,6},{9,8},{10,9},{11,10},{12... | collective-permute-start | bytes 5406728 | tf_op jit(solution)/shard_map/ppermute | solution.py:350
  40.3 19.2 %collective-permute-start.3 = (f32[5,3,40,256]{3,2,1,0:T(8,128)}, f32[5,3,40,256]{3,2,1,0:T(8,128)}, u32[]{:S(2)}, u32[]{:S(2)}) collective-permute-start(f32[5,3,40,256]{3,2,1,0:T(8,128)} %fusion), channel_id=1, source_target_pairs={{8,0},{16,8},{24,16},{9,1},{17,9},{25,17},{10,2},{18,10},{26,18},{... | collective-permute-start | bytes 1843208 | tf_op jit(solution)/shard_map/ppermute | solution.py:350
  46.9 47.6 %collective-permute-start.8 = (f32[5,3,40,256]{3,2,1,0:T(8,128)}, f32[5,3,40,256]{3,2,1,0:T(8,128)}, u32[]{:S(2)}, u32[]{:S(2)}) collective-permute-start(f32[5,3,40,256]{3,2,1,0:T(8,128)} %select_maximum_fusion.3), channel_id=1, source_target_pairs={{0,8},{8,16},{16,24},{1,9},{9,17},{17,25},{2,10},{10,18},{18,26},{... | collective-permute-start | bytes 1843208 | tf_op jit(solution)/shard_map/ppermute | solution.py:349
  56.0 39.8 %collective-permute-start.9 = (f32[5,3,40,256]{3,2,1,0:T(8,128)}, f32[5,3,40,256]{3,2,1,0:T(8,128)}, u32[]{:S(2)}, u32[]{:S(2)}) collective-permute-start(f32[5,3,40,256]{3,2,1,0:T(8,128)} %select_maximum_fusion.2), channel_id=1, source_target_pairs={{8,0},{16,8},{24,16},{9,1},{17,9},{25,17},{10,2},{18,10},{26,18},{... | collective-permute-start | bytes 1843208 | tf_op jit(solution)/shard_map/ppermute | solution.py:350
  70.8 74.5 %collective-permute-start.6 = (f32[5,11,40,256]{3,2,1,0:T(8,128)}, f32[5,11,40,256]{3,2,1,0:T(8,128)S(1)}, u32[]{:S(2)}, u32[]{:S(2)}) collective-permute-start(f32[5,11,40,256]{3,2,1,0:T(8,128)} %select_maximum_fusion.1), channel_id=1, source_target_pairs={{0,8},{8,16},{16,24},{1,9},{9,17},{17,25},{2,10},{10,18},{18,26},{... | collective-permute-start | bytes 6758408 | tf_op jit(solution)/shard_map/ppermute | solution.py:349
  73.7 73.1 %collective-permute-start.7 = (f32[5,11,40,256]{3,2,1,0:T(8,128)}, f32[5,11,40,256]{3,2,1,0:T(8,128)}, u32[]{:S(2)}, u32[]{:S(2)}) collective-permute-start(f32[5,11,40,256]{3,2,1,0:T(8,128)} %select_maximum_fusion), channel_id=1, source_target_pairs={{8,0},{16,8},{24,16},{9,1},{17,9},{25,17},{10,2},{18,10},{26,18},{... | collective-permute-start | bytes 6758408 | tf_op jit(solution)/shard_map/ppermute | solution.py:350
  102.4 27.9 %collective-permute-start.14 = (f32[2,8,32,128]{3,2,1,0:T(8,128)}, f32[2,8,32,128]{3,2,1,0:T(8,128)S(1)}, u32[]{:S(2)}, u32[]{:S(2)}) collective-permute-start(f32[2,8,32,128]{3,2,1,0:T(8,128)} %get-tuple-element.66), channel_id=1, source_target_pairs={{0,5},{1,4},{2,7},{3,6},{4,1},{5,0},{6,3},{7,2},{8,13},{9,12},{10,... | collective-permute-start | bytes 786440 | tf_op jit(solution)/shard_map/ppermute | solution.py:453
  108.7 22.3 %collective-permute-start.15 = (f32[2,8,32,128]{3,2,1,0:T(8,128)}, f32[2,8,32,128]{3,2,1,0:T(8,128)S(1)}, u32[]{:S(2)}, u32[]{:S(2)}) collective-permute-start(f32[2,8,32,128]{3,2,1,0:T(8,128)} %get-tuple-element.67), channel_id=1, source_target_pairs={{0,6},{1,7},{2,4},{3,5},{4,2},{5,3},{6,0},{7,1},{8,14},{9,15},{10,... | collective-permute-start | bytes 786440 | tf_op jit(solution)/shard_map/ppermute | solution.py:453
  109.4 24.7 %collective-permute-start.16 = (f32[2,8,32,128]{3,2,1,0:T(8,128)}, f32[2,8,32,128]{3,2,1,0:T(8,128)}, u32[]{:S(2)}, u32[]{:S(2)}) collective-permute-start(f32[2,8,32,128]{3,2,1,0:T(8,128)} %get-tuple-element.68), channel_id=1, source_target_pairs={{0,7},{1,6},{2,5},{3,4},{4,3},{5,2},{6,1},{7,0},{8,15},{9,14},{10,... | collective-permute-start | bytes 786440 | tf_op jit(solution)/shard_map/ppermute | solution.py:453
  134.2 37.9 %collective-permute-start.19 = (f32[3,8,32,128]{3,2,1,0:T(8,128)}, f32[3,8,32,128]{3,2,1,0:T(8,128)S(1)}, u32[]{:S(2)}, u32[]{:S(2)}) collective-permute-start(f32[3,8,32,128]{3,2,1,0:T(8,128)} %get-tuple-element.75), channel_id=1, source_target_pairs={{0,3},{1,2},{2,1},{3,0},{4,7},{5,6},{6,5},{7,4},{8,11},{9,10},{10,... | collective-permute-start | bytes 1179656 | tf_op jit(solution)/shard_map/ppermute | solution.py:453
  141.7 31.5 %collective-permute-start.20 = (f32[3,8,32,128]{3,2,1,0:T(8,128)}, f32[3,8,32,128]{3,2,1,0:T(8,128)S(1)}, u32[]{:S(2)}, u32[]{:S(2)}) collective-permute-start(f32[3,8,32,128]{3,2,1,0:T(8,128)} %get-tuple-element.76), channel_id=1, source_target_pairs={{0,4},{1,5},{2,6},{3,7},{4,0},{5,1},{6,2},{7,3},{8,12},{9,13},{10,... | collective-permute-start | bytes 1179656 | tf_op jit(solution)/shard_map/ppermute | solution.py:453
  142.6 35.8 %collective-permute-start.21 = (f32[3,8,32,128]{3,2,1,0:T(8,128)}, f32[3,8,32,128]{3,2,1,0:T(8,128)}, u32[]{:S(2)}, u32[]{:S(2)}) collective-permute-start(f32[3,8,32,128]{3,2,1,0:T(8,128)} %get-tuple-element.77), channel_id=1, source_target_pairs={{0,5},{1,4},{2,7},{3,6},{4,1},{5,0},{6,3},{7,2},{8,13},{9,12},{10,... | collective-permute-start | bytes 1179656 | tf_op jit(solution)/shard_map/ppermute | solution.py:453
  145.3 34.5 %collective-permute-start.22 = (f32[3,8,32,128]{3,2,1,0:T(8,128)}, f32[3,8,32,128]{3,2,1,0:T(8,128)}, u32[]{:S(2)}, u32[]{:S(2)}) collective-permute-start(f32[3,8,32,128]{3,2,1,0:T(8,128)} %get-tuple-element.78), channel_id=1, source_target_pairs={{0,6},{1,7},{2,4},{3,5},{4,2},{5,3},{6,0},{7,1},{8,14},{9,15},{10,... | collective-permute-start | bytes 1179656 | tf_op jit(solution)/shard_map/ppermute | solution.py:453
  146.7 33.0 %collective-permute-start.23 = (f32[3,8,32,128]{3,2,1,0:T(8,128)}, f32[3,8,32,128]{3,2,1,0:T(8,128)}, u32[]{:S(2)}, u32[]{:S(2)}) collective-permute-start(f32[3,8,32,128]{3,2,1,0:T(8,128)} %get-tuple-element.79), channel_id=1, source_target_pairs={{0,7},{1,6},{2,5},{3,4},{4,3},{5,2},{6,1},{7,0},{8,15},{9,14},{10,... | collective-permute-start | bytes 1179656 | tf_op jit(solution)/shard_map/ppermute | solution.py:453
  178.4 39.2 %collective-permute-start.26 = (f32[4,8,32,128]{3,2,1,0:T(8,128)}, f32[4,8,32,128]{3,2,1,0:T(8,128)S(1)}, u32[]{:S(2)}, u32[]{:S(2)}) collective-permute-start(f32[4,8,32,128]{3,2,1,0:T(8,128)} %get-tuple-element.87), channel_id=1, source_target_pairs={{0,3},{1,2},{2,1},{3,0},{4,7},{5,6},{6,5},{7,4},{8,11},{9,10},{10,... | collective-permute-start | bytes 1572872 | tf_op jit(solution)/shard_map/ppermute | solution.py:453
  179.8 38.2 %collective-permute-start.27 = (f32[4,8,32,128]{3,2,1,0:T(8,128)}, f32[4,8,32,128]{3,2,1,0:T(8,128)S(1)}, u32[]{:S(2)}, u32[]{:S(2)}) collective-permute-start(f32[4,8,32,128]{3,2,1,0:T(8,128)} %get-tuple-element.88), channel_id=1, source_target_pairs={{0,4},{1,5},{2,6},{3,7},{4,0},{5,1},{6,2},{7,3},{8,12},{9,13},{10,... | collective-permute-start | bytes 1572872 | tf_op jit(solution)/shard_map/ppermute | solution.py:453
  179.8 47.9 %collective-permute-start.28 = (f32[4,8,32,128]{3,2,1,0:T(8,128)}, f32[4,8,32,128]{3,2,1,0:T(8,128)S(1)}, u32[]{:S(2)}, u32[]{:S(2)}) collective-permute-start(f32[4,8,32,128]{3,2,1,0:T(8,128)} %get-tuple-element.89), channel_id=1, source_target_pairs={{0,5},{1,4},{2,7},{3,6},{4,1},{5,0},{6,3},{7,2},{8,13},{9,12},{10,... | collective-permute-start | bytes 1572872 | tf_op jit(solution)/shard_map/ppermute | solution.py:453
  189.6 38.1 %collective-permute-start.29 = (f32[4,8,32,128]{3,2,1,0:T(8,128)}, f32[4,8,32,128]{3,2,1,0:T(8,128)}, u32[]{:S(2)}, u32[]{:S(2)}) collective-permute-start(f32[4,8,32,128]{3,2,1,0:T(8,128)} %get-tuple-element.90), channel_id=1, source_target_pairs={{0,6},{1,7},{2,4},{3,5},{4,2},{5,3},{6,0},{7,1},{8,14},{9,15},{10,... | collective-permute-start | bytes 1572872 | tf_op jit(solution)/shard_map/ppermute | solution.py:453
  190.6 37.3 %collective-permute-start.30 = (f32[4,8,32,128]{3,2,1,0:T(8,128)}, f32[4,8,32,128]{3,2,1,0:T(8,128)}, u32[]{:S(2)}, u32[]{:S(2)}) collective-permute-start(f32[4,8,32,128]{3,2,1,0:T(8,128)} %get-tuple-element.91), channel_id=1, source_target_pairs={{0,7},{1,6},{2,5},{3,4},{4,3},{5,2},{6,1},{7,0},{8,15},{9,14},{10,... | collective-permute-start | bytes 1572872 | tf_op jit(solution)/shard_map/ppermute | solution.py:453
  217.6 22.2 %collective-permute-start.38 = (f32[4,8,32,128]{3,2,1,0:T(8,128)}, f32[4,8,32,128]{3,2,1,0:T(8,128)S(1)}, u32[]{:S(2)}, u32[]{:S(2)}) collective-permute-start(f32[4,8,32,128]{3,2,1,0:T(8,128)} %get-tuple-element.105), channel_id=1, source_target_pairs={{0,1},{1,0},{2,3},{3,2},{4,5},{5,4},{6,7},{7,6},{8,9},{9,8},{10,11... | collective-permute-start | bytes 1572872 | tf_op jit(solution)/shard_map/ppermute | solution.py:453
  218.0 22.8 %collective-permute-start.39 = (f32[4,8,32,128]{3,2,1,0:T(8,128)}, f32[4,8,32,128]{3,2,1,0:T(8,128)S(1)}, u32[]{:S(2)}, u32[]{:S(2)}) collective-permute-start(f32[4,8,32,128]{3,2,1,0:T(8,128)} %get-tuple-element.106), channel_id=1, source_target_pairs={{0,2},{1,3},{2,0},{3,1},{4,6},{5,7},{6,4},{7,5},{8,10},{9,11},{10,... | collective-permute-start | bytes 1572872 | tf_op jit(solution)/shard_map/ppermute | solution.py:453
  227.7 33.9 %collective-permute-start.40 = (f32[4,8,32,128]{3,2,1,0:T(8,128)}, f32[4,8,32,128]{3,2,1,0:T(8,128)S(1)}, u32[]{:S(2)}, u32[]{:S(2)}) collective-permute-start(f32[4,8,32,128]{3,2,1,0:T(8,128)} %get-tuple-element.107), channel_id=1, source_target_pairs={{0,3},{1,2},{2,1},{3,0},{4,7},{5,6},{6,5},{7,4},{8,11},{9,10},{10,... | collective-permute-start | bytes 1572872 | tf_op jit(solution)/shard_map/ppermute | solution.py:453
  227.7 34.7 %collective-permute-start.41 = (f32[4,8,32,128]{3,2,1,0:T(8,128)}, f32[4,8,32,128]{3,2,1,0:T(8,128)S(1)}, u32[]{:S(2)}, u32[]{:S(2)}) collective-permute-start(f32[4,8,32,128]{3,2,1,0:T(8,128)} %get-tuple-element.108), channel_id=1, source_target_pairs={{0,4},{1,5},{2,6},{3,7},{4,0},{5,1},{6,2},{7,3},{8,12},{9,13},{10,... | collective-permute-start | bytes 1572872 | tf_op jit(solution)/shard_map/ppermute | solution.py:453
  228.5 46.8 %collective-permute-start.42 = (f32[4,8,32,128]{3,2,1,0:T(8,128)}, f32[4,8,32,128]{3,2,1,0:T(8,128)S(1)}, u32[]{:S(2)}, u32[]{:S(2)}) collective-permute-start(f32[4,8,32,128]{3,2,1,0:T(8,128)} %get-tuple-element.109), channel_id=1, source_target_pairs={{0,5},{1,4},{2,7},{3,6},{4,1},{5,0},{6,3},{7,2},{8,13},{9,12},{10,... | collective-permute-start | bytes 1572872 | tf_op jit(solution)/shard_map/ppermute | solution.py:453
  239.8 36.2 %collective-permute-start.43 = (f32[4,8,32,128]{3,2,1,0:T(8,128)}, f32[4,8,32,128]{3,2,1,0:T(8,128)S(1)}, u32[]{:S(2)}, u32[]{:S(2)}) collective-permute-start(f32[4,8,32,128]{3,2,1,0:T(8,128)} %get-tuple-element.110), channel_id=1, source_target_pairs={{0,6},{1,7},{2,4},{3,5},{4,2},{5,3},{6,0},{7,1},{8,14},{9,15},{10,... | collective-permute-start | bytes 1572872 | tf_op jit(solution)/shard_map/ppermute | solution.py:453
  240.8 35.7 %collective-permute-start.44 = (f32[4,8,32,128]{3,2,1,0:T(8,128)}, f32[4,8,32,128]{3,2,1,0:T(8,128)S(1)}, u32[]{:S(2)}, u32[]{:S(2)}) collective-permute-start(f32[4,8,32,128]{3,2,1,0:T(8,128)} %get-tuple-element.111), channel_id=1, source_target_pairs={{0,7},{1,6},{2,5},{3,4},{4,3},{5,2},{6,1},{7,0},{8,15},{9,14},{10,... | collective-permute-start | bytes 1572872 | tf_op jit(solution)/shard_map/ppermute | solution.py:453
  276.5 36.0 %collective-permute-start.35 = (f32[3,8,32,128]{3,2,1,0:T(8,128)}, f32[3,8,32,128]{3,2,1,0:T(8,128)}, u32[]{:S(2)}, u32[]{:S(2)}) collective-permute-start(f32[3,8,32,128]{3,2,1,0:T(8,128)} %get-tuple-element.101), channel_id=1, source_target_pairs={{0,5},{1,4},{2,7},{3,6},{4,1},{5,0},{6,3},{7,2},{8,13},{9,12},{10,... | collective-permute-start | bytes 1179656 | tf_op jit(solution)/shard_map/ppermute | solution.py:453
  278.6 33.9 %collective-permute-start.36 = (f32[3,8,32,128]{3,2,1,0:T(8,128)}, f32[3,8,32,128]{3,2,1,0:T(8,128)}, u32[]{:S(2)}, u32[]{:S(2)}) collective-permute-start(f32[3,8,32,128]{3,2,1,0:T(8,128)} %get-tuple-element.102), channel_id=1, source_target_pairs={{0,6},{1,7},{2,4},{3,5},{4,2},{5,3},{6,0},{7,1},{8,14},{9,15},{10,... | collective-permute-start | bytes 1179656 | tf_op jit(solution)/shard_map/ppermute | solution.py:453
  278.7 33.8 %collective-permute-start.37 = (f32[3,8,32,128]{3,2,1,0:T(8,128)}, f32[3,8,32,128]{3,2,1,0:T(8,128)}, u32[]{:S(2)}, u32[]{:S(2)}) collective-permute-start(f32[3,8,32,128]{3,2,1,0:T(8,128)} %get-tuple-element.103), channel_id=1, source_target_pairs={{0,7},{1,6},{2,5},{3,4},{4,3},{5,2},{6,1},{7,0},{8,15},{9,14},{10,... | collective-permute-start | bytes 1179656 | tf_op jit(solution)/shard_map/ppermute | solution.py:453
  (48 other events, 625.9 us)
